TPU v7x, 128 devices: a whole 4x4x4 slice. The times are simulated.
128 devices in a mesh: fsdp: 32 (over z, y, core), tensor: 4 (over x).
Axes of the slice: x: 4, y: 4, z: 4, core: 2. Of those that a mesh axis runs over, the one named last changes fastest.
Arguments:
- gradient: float32 [16, 512, 8192], P(None, 'fsdp', 'tensor'), may hold values from -1500 to 1500
- owner: int32 [16, 16], P(None, 'tensor'), may hold values from 0 to 31, as said below
- slot: int32 [16, 16], P(None, 'tensor'), may hold values from 0 to 3
- left_gram: float32 [512, 512, 512], P(('fsdp', 'tensor')), may hold values from -1 to 1, as said below
- right_gram: float32 [512, 512, 512], P(('fsdp', 'tensor')), may hold values from -1 to 1, as said below
- left_root: bfloat16 [512, 512, 512], P(('fsdp', 'tensor')), may hold values from -1 to 4, as said below
- right_root: bfloat16 [512, 512, 512], P(('fsdp', 'tensor')), may hold values from -1 to 4, as said below
Outputs:
- left_gram_new: float32 [512, 512, 512], P(('fsdp', 'tensor'))
- right_gram_new: float32 [512, 512, 512], P(('fsdp', 'tensor'))
- update: bfloat16 [16, 512, 8192], P(None, 'fsdp', 'tensor')
Inputs may be any that keep to these rules, and one draw needn't show every extreme that they name: In every tensor index, no two blocks share an owner and a slot, and some owner holds 4 blocks. `left_gram`: Symmetric. `right_gram`: Symmetric. `left_root`: Symmetric. `right_root`: Symmetric.
All inputs are finite; a program needn't handle non-finite values.
Results may differ from a plain program's by a relative error of at most 0.015.
Values may be sent and summed in bfloat16 or wider, within the bound.
A program may use at most 128 MiB of HBM per device.

v0:
```python
import functools

import jax
import jax.numpy as jnp
from jax import lax
from jax.experimental import pallas as pl
from jax.experimental.pallas import tpu as pltpu
from jax.sharding import PartitionSpec as P

clip_rms = 0.05
eps_norm = 1e-06
MESH = pl.DeviceIdType.MESH


def exchange_kernel(
    entry_count, owners, tensors, slots, rows, size,
    owner_hbm, slot_hbm, grad_hbm, lroot_hbm, rroot_hbm, lgram_hbm, rgram_hbm,
    left_new, right_new, returned, scale,
    owner_ref, slot_ref, grad, lroot, rroot, own, give, take, arrived, results, back_take,
    table_v, table_s, side_sums, sums, halves, total,
    local_sem, table_sem, side_send, side_recv, sum_send, sum_recv, half_send, half_recv, total_send, total_recv,
    give_send, give_recv, go_send, go_recv, back_give_send, back_give_recv, back_send, back_recv,
):
    me = lax.axis_index("fsdp")
    side = lax.axis_index("tensor")
    per_row, row_blocks = owner_ref.shape
    positions = owners * slots
    chips = owners // 2
    chip, core = me // 2, me % 2
    mate = chip * 2 + 1 - core

    barrier = pltpu.get_barrier_semaphore()
    for i in range(1, chips):
        pl.semaphore_signal(
            barrier, inc=1, device_id={"fsdp": (chip + i) % chips * 2 + core}, device_id_type=MESH
        )
    pl.semaphore_signal(barrier, inc=1, device_id={"fsdp": mate}, device_id_type=MESH)

    speaker = 5

    @pl.when(chip == speaker)
    def _():
        for t in range(1, tensors):
            pl.semaphore_signal(
                barrier, inc=1, device_id={"tensor": (side + t) % tensors}, device_id_type=MESH
            )

    load_left = pltpu.make_async_copy(lroot_hbm, lroot, local_sem.at[0])
    load_right = pltpu.make_async_copy(rroot_hbm, rroot, local_sem.at[1])
    load_lgram = pltpu.make_async_copy(lgram_hbm, left_new, local_sem.at[2])
    load_rgram = pltpu.make_async_copy(rgram_hbm, right_new, local_sem.at[3])
    load_grad = [
        pltpu.make_async_copy(
            grad_hbm.at[:, :, pl.ds(c * size, size)],
            grad.at[pl.ds(c * row_blocks, row_blocks)],
            local_sem.at[4 + c],
        )
        for c in range(per_row)
    ]
    load_tables = [
        pltpu.make_async_copy(owner_hbm, owner_ref, local_sem.at[4 + per_row]),
        pltpu.make_async_copy(slot_hbm, slot_ref, local_sem.at[5 + per_row]),
    ]
    for load in load_tables + load_grad:
        load.start()

    for load in load_tables:
        load.wait()
    target = owner_ref[...] * slots + slot_ref[...]
    lanes = lax.broadcasted_iota(jnp.int32, (row_blocks, positions), 1)
    block_rows = lax.broadcasted_iota(jnp.int32, (row_blocks, positions), 0)
    source = jnp.zeros((row_blocks, positions), jnp.int32)
    filled = jnp.zeros((row_blocks, positions), jnp.float32)
    target = target.T
    for c in range(per_row):
        hit = target[:, c : c + 1] == lanes
        source = jnp.where(hit, block_rows + c * row_blocks, source)
        filled = jnp.where(hit, 1.0, filled)
    table_v[...] = jnp.max(source, axis=0, keepdims=True)
    filled = jnp.max(filled, axis=0, keepdims=True)
    load_table = pltpu.make_async_copy(table_v, table_s, table_sem)
    load_table.start()

    for load in load_grad:
        load.wait()
    load_table.wait()
    for load in (load_left, load_right, load_lgram, load_rgram):
        load.start()

    def piece(s, o):
        return grad[table_s[0, o * slots + s]].astype(jnp.bfloat16)

    def rows_of(f):
        return pl.ds(pl.multiple_of(f * rows, rows), rows)

    def chip_at(d):
        return (chip // 4 + d // 4) % 4 * 4 + (chip % 4 + d % 4) % 4

    def send(src, dst, send_sem, recv_sem, **to):
        copy = pltpu.make_async_remote_copy(
            src_ref=src, dst_ref=dst, send_sem=send_sem, recv_sem=recv_sem,
            device_id=to, device_id_type=MESH,
        )
        copy.start()
        return copy

    def all_of(some, send_sem, recv_sem):
        return pltpu.make_async_remote_copy(
            src_ref=some, dst_ref=some, send_sem=send_sem, recv_sem=recv_sem,
            device_id={"fsdp": mate}, device_id_type=MESH,
        )

    def fill_give(s):
        def fill(k, carry):
            give[s, k] = piece(s, k * 2 + 1 - core)
            return carry

        lax.fori_loop(0, chips, fill, 0)

    def send_give(s):
        send(give.at[s], take.at[s], give_send.at[s], give_recv.at[s], fsdp=mate)

    def send_own(s):
        def go(d, carry):
            k = chip_at(d)
            o = k * 2 + core
            own[s, k] = piece(s, o)
            send(own.at[s, k], arrived.at[s, rows_of(me), :], go_send.at[s], go_recv.at[s], fsdp=o)
            return carry

        lax.fori_loop(1, chips, go, 0)
        arrived[s, rows_of(me), :] = piece(s, me)

    def send_take(s):
        all_of(take.at[s], give_send.at[s], give_recv.at[s]).wait_recv()

        def go(d, carry):
            k = chip_at(d)
            send(
                take.at[s, k], arrived.at[s, rows_of(mate), :], go_send.at[s], go_recv.at[s],
                fsdp=k * 2 + core,
            )
            return carry

        lax.fori_loop(1, chips, go, 0)
        arrived[s, rows_of(mate), :] = take[s, chip]

    fill_give(0)
    pl.semaphore_wait(barrier, chips + jnp.where(chip == speaker, tensors - 1, 0))

    send_give(0)
    send_own(0)
    fill_give(1)
    send_give(1)

    def square(b, total):
        block = grad[b]
        return total + block * block

    own_sum = lax.fori_loop(0, row_blocks * per_row, square, jnp.zeros((rows, size), jnp.float32))
    own_sum = sum(own_sum[:, k : k + 128] for k in range(0, size, 128))
    sums[chip] = jnp.sum(own_sum, axis=0, keepdims=True)

    def send_sum(d, carry):
        send(sums.at[chip], sums.at[chip], sum_send, sum_recv, fsdp=chip_at(d) * 2 + core)
        return carry

    lax.fori_loop(1, chips, send_sum, 0)
    send_take(0)
    send_own(1)
    fill_give(2)
    send_give(2)
    send_take(1)
    sum_all = all_of(sums.at[pl.ds(0, chips - 1)], sum_send, sum_recv)
    sum_all.wait_recv()
    halves[core] = jnp.sum(sums[...], axis=0)
    half = send(halves.at[core], halves.at[core], half_send, half_recv, fsdp=mate)
    send_own(2)
    fill_give(3)
    send_give(3)
    half.wait_recv()
    side_sums[side] = halves[0] + halves[1]
    side_all = all_of(side_sums.at[pl.ds(0, tensors - 1)], side_send, side_recv)

    @pl.when(chip == speaker)
    def _():
        for t in range(1, tensors):
            send(
                side_sums.at[side], side_sums.at[side], side_send, side_recv,
                tensor=(side + t) % tensors,
            )

    send_take(2)
    send_own(3)
    send_take(3)

    load_left.wait()
    load_right.wait()

    def send_back(s, kind):
        def back(d, carry):
            k = chip_at(d)
            src, owner = (results.at[s, k, core], me) if kind == "own" else (back_take.at[s, k], mate)
            send(
                src, returned.at[owner * slots + s], back_send.at[s], back_recv.at[s],
                fsdp=k * 2 + core,
            )
            return carry

        lax.fori_loop(1, chips, back, 0)

    def wait_back_take(s):
        all_of(back_take.at[s], back_give_send.at[s], back_give_recv.at[s]).wait_recv()
        returned[mate * slots + s] = back_take[s, chip]

    def spread_total():
        @pl.when(chip == speaker)
        def _():
            side_all.wait_recv()
            total[0] = jnp.sum(side_sums[...], axis=0)

            def send_total(d, carry):
                send(total.at[0], total.at[0], total_send, total_recv, fsdp=chip_at(d) * 2 + core)
                return carry

            lax.fori_loop(1, chips, send_total, 0)

    some = returned.at[pl.ds(0, 2 * chips - 2)]
    for s in range(slots):
        all_of(some, go_send.at[s], go_recv.at[s]).wait_recv()
        left_side = jnp.dot(
            lroot[s], arrived[s], preferred_element_type=jnp.float32
        ).astype(jnp.bfloat16)
        product = jnp.dot(left_side, rroot[s], preferred_element_type=jnp.float32)
        results[s] = product.astype(jnp.bfloat16).reshape(chips, 2, rows, size)
        send(
            results.at[s, :, 1 - core], back_take.at[s], back_give_send.at[s], back_give_recv.at[s],
            fsdp=mate,
        )
        returned[me * slots + s] = results[s, chip, core]
        send_back(s, "own")
        if s > 0:
            wait_back_take(s - 1)
            send_back(s - 1, "mate")
        else:
            spread_total()
    wait_back_take(slots - 1)
    send_back(slots - 1, "mate")

    @pl.when(chip != speaker)
    def _():
        all_of(total.at[0], total_send, total_recv).wait_recv()

    grand_sum = jnp.sum(total[0], axis=1, keepdims=True)
    factor = clip_rms / jnp.sqrt(grand_sum / entry_count + eps_norm)
    scale[...] = jnp.broadcast_to(factor, (1, 128))
    lane = lax.broadcasted_iota(jnp.int32, (1, positions), 1)
    gain = []
    for s in range(slots):
        mine = jnp.sum(jnp.where(lane == me * slots + s, filled, 0.0), axis=1, keepdims=True)
        gain.append(factor * factor * mine)
    load_lgram.wait()
    load_rgram.wait()
    for s in range(slots):
        g = arrived[s]
        left_new[s] += gain[s] * lax.dot_general(
            g, g, (((1,), (1,)), ((), ())), preferred_element_type=jnp.float32
        )
        right_new[s] += gain[s] * lax.dot_general(
            g, g, (((0,), (0,)), ((), ())), preferred_element_type=jnp.float32
        )

    for s in range(slots):
        all_of(some, back_send.at[s], back_recv.at[s]).wait_recv()

    @pl.when(chip == speaker)
    def _():
        side_all.wait_send()
        all_of(sums.at[pl.ds(0, chips - 1)], total_send, total_recv).wait_send()

    sum_all.wait_send()
    half.wait_send()
    for s in range(slots):
        all_of(take.at[s], give_send.at[s], give_recv.at[s]).wait_send()
        all_of(take.at[s], back_give_send.at[s], back_give_recv.at[s]).wait_send()
        all_of(some, go_send.at[s], go_recv.at[s]).wait_send()
        all_of(some, back_send.at[s], back_recv.at[s]).wait_send()


def finish_kernel(
    slots, owner_hbm, slot_hbm, left, right, returned, scale, left_new, right_new, update,
    owner, slot, placed, sems, table_sems,
):
    load_owner = pltpu.make_async_copy(owner_hbm, owner, table_sems.at[0])
    load_slot = pltpu.make_async_copy(slot_hbm, slot, table_sems.at[1])
    load_owner.start()
    load_slot.start()
    per_row, row_blocks = owner.shape
    size = left.shape[-1]
    copies = []
    for s in range(slots):
        for ref, new in ((left, left_new), (right, right_new)):
            copies.append(pltpu.make_async_copy(ref.at[s], new.at[s], sems.at[len(copies)]))
            copies[-1].start()

    factor = scale[0:1, 0:1]

    def place(r, carry):
        for c in range(per_row):
            block = returned[owner[c, r] * slots + slot[c, r]].astype(jnp.float32)
            placed[r, :, c * size : (c + 1) * size] = (block * factor).astype(placed.dtype)
        return carry

    load_owner.wait()
    load_slot.wait()
    quarter = row_blocks // 4
    for k in range(0, row_blocks, quarter):
        lax.fori_loop(k, k + quarter, place, 0)
        part = pl.ds(k, quarter)
        copies.append(pltpu.make_async_copy(placed.at[part], update.at[part], sems.at[len(copies)]))
        copies[-1].start()
    for copy in copies:
        copy.wait()


def per_device(gradient, owner, slot, left_gram, right_gram, left_root, right_root):
    row_blocks, rows, col_count = gradient.shape
    slots, size, _ = left_gram.shape
    owners, tensors = lax.axis_size("fsdp"), lax.axis_size("tensor")
    positions, per_row, chips = owners * slots, col_count // size, owners // 2
    entry_count = float(row_blocks * rows * col_count * owners * tensors)
    vmem = pl.BlockSpec(memory_space=pltpu.VMEM)
    dma = pltpu.SemaphoreType.DMA
    bf16, f32, i32 = jnp.bfloat16, jnp.float32, jnp.int32
    hbm = pl.BlockSpec(memory_space=pltpu.HBM)
    owner, slot = owner.T, slot.T
    big = [
        pltpu.with_memory_space_constraint(x, pltpu.HBM)
        for x in (owner, slot, gradient, left_root, right_root, left_gram, right_gram)
    ]
    left, right, returned, scale = pl.pallas_call(
        functools.partial(exchange_kernel, entry_count, owners, tensors, slots, rows, size),
        out_shape=(
            pltpu.VMEM((slots, size, size), f32),
            pltpu.VMEM((slots, size, size), f32),
            pltpu.VMEM((positions, rows, size), bf16),
            pltpu.VMEM((1, 128), f32),
        ),
        in_specs=[hbm] * 7,
        out_specs=(vmem, vmem, vmem, vmem),
        scratch_shapes=[
            pltpu.VMEM((per_row, row_blocks), i32),
            pltpu.VMEM((per_row, row_blocks), i32),
            pltpu.VMEM((row_blocks * per_row, rows, size), f32),
            pltpu.VMEM((slots, size, size), bf16),
            pltpu.VMEM((slots, size, size), bf16),
            pltpu.VMEM((slots, chips, rows, size), bf16),
            pltpu.VMEM((slots, chips, rows, size), bf16),
            pltpu.VMEM((slots, chips, rows, size), bf16),
            pltpu.VMEM((slots, size, size), bf16),
            pltpu.VMEM((slots, chips, 2, rows, size), bf16),
            pltpu.VMEM((slots, chips, rows, size), bf16),
            pltpu.VMEM((1, positions), i32),
            pltpu.SMEM((1, positions), i32),
            pltpu.VMEM((tensors, 1, 128), f32),
            pltpu.VMEM((chips, 1, 128), f32),
            pltpu.VMEM((2, 1, 128), f32),
            pltpu.VMEM((1, 1, 128), f32),
            dma((6 + per_row,)), *[dma] * 9, *[dma((slots,))] * 8,
        ],
        compiler_params=pltpu.CompilerParams(
            collective_id=0, has_side_effects=True, vmem_limit_bytes=32 * 2**20
        ),
        cost_estimate=pl.CostEstimate(
            flops=8 * slots * size**3, bytes_accessed=24 * 2**20, transcendentals=0
        ),
        name="exchange",
    )(*big)
    return pl.pallas_call(
        functools.partial(finish_kernel, slots),
        out_shape=(
            jax.ShapeDtypeStruct(left_gram.shape, f32),
            jax.ShapeDtypeStruct(right_gram.shape, f32),
            jax.ShapeDtypeStruct(gradient.shape, bf16),
        ),
        in_specs=[hbm, hbm, vmem, vmem, vmem, vmem],
        out_specs=(hbm, hbm, hbm),
        scratch_shapes=[
            pltpu.SMEM(owner.shape, i32),
            pltpu.SMEM(owner.shape, i32),
            pltpu.VMEM(gradient.shape, bf16),
            dma((2 * slots + 4,)),
            dma((2,)),
        ],
        compiler_params=pltpu.CompilerParams(vmem_limit_bytes=24 * 2**20),
        cost_estimate=pl.CostEstimate(flops=0, bytes_accessed=9 * 2**20, transcendentals=0),
        name="finish",
    )(*big[:2], left, right, returned, scale)


def solution(mesh):
    return jax.shard_map(
        per_device,
        mesh=mesh,
        in_specs=(
            P(None, "fsdp", "tensor"),
            P(None, "tensor"),
            P(None, "tensor"),
            P(("fsdp", "tensor"), None, None),
            P(("fsdp", "tensor"), None, None),
            P(("fsdp", "tensor"), None, None),
            P(("fsdp", "tensor"), None, None),
        ),
        out_specs=(
            P(("fsdp", "tensor"), None, None),
            P(("fsdp", "tensor"), None, None),
            P(None, "fsdp", "tensor"),
        ),
        check_vma=False,
    )
```

profile of v0, /device:TPU:0, one launch (start us, length us, event | category | flops | bytes accessed | tf_op | source)
XLA Modules:
  0.0 59.1 jit_solution(17871176338938941875)
XLA Ops:
  0.6 54.7 %exchange.1 = (f32[4,512,512]{2,1,0:T(8,128)S(1)}, f32[4,512,512]{2,1,0:T(8,128)S(1)}, bf16[128,16,512]{2,1,0:T(8,128)(2,1)S(1)}, f32[1,128]{1,0:T(1,128)S(1)}) custom-call(s32[4,16]{1,0:T(4,128)} %bitcast.2, s32[4,16]{1,0:T(4,128)} %bitcast.4, f32[16,16,2048]{2,1,0:T(8,128)} %grad_hbm.1, bf16[4,512,512]{2,1,0:T(8,128)(2,1)} %lroot_hbm.1, ...), custom_call_target="tpu_custom_call" | custom-call | flops 4294967296 | bytes 25165824 | tf_op jit(solution)/shard_map/exchange/pallas_call | solution.py:341
  55.4 3.7 %finish.1 = (f32[4,512,512]{2,1,0:T(8,128)}, f32[4,512,512]{2,1,0:T(8,128)}, bf16[16,16,2048]{2,1,0:T(8,128)(2,1)}) custom-call(s32[4,16]{1,0:T(4,128)} %bitcast.3, s32[4,16]{1,0:T(4,128)} %bitcast.5, f32[4,512,512]{2,1,0:T(8,128)S(1)} %get-tuple-element.7.left, f32[4,512,512]{2,1,0:T(8,128)S(1)} %get-tuple-element.8.right, ...), custom_call_target="tpu_custom_call" | custom-call | bytes 9437184 | tf_op jit(solution)/shard_map/finish/pallas_call | solution.py:379
where the time goes:
time: 59.3 us; the launch traced here: 59.1 us
  Pallas kernels  58.4 us (98%)
  between operations  0.64 us (1%)
    pallas_call x1, Pallas kernels, per_device(): pl.pallas_call(functools.partial(exchange_kernel, entry_count, owners, te...  54.7 us
    pallas_call x1, Pallas kernels, per_device(): pl.pallas_call(functools.partial(finish_kernel, slots), out_shape=(jax.Sh...  3.71 us

commit v1 on v0

--- a/solution.py
+++ b/solution.py
@@ -94,6 +94,7 @@
         return pl.ds(pl.multiple_of(f * rows, rows), rows)
 
     def chip_at(d):
+        d = jnp.where(core == 0, d, 16 - d)
         return (chip // 4 + d // 4) % 4 * 4 + (chip % 4 + d % 4) % 4
 
     def send(src, dst, send_sem, recv_sem, **to):
@@ -238,11 +239,11 @@
             fsdp=mate,
         )
         returned[me * slots + s] = results[s, chip, core]
-        send_back(s, "own")
         if s > 0:
             wait_back_take(s - 1)
             send_back(s - 1, "mate")
-        else:
+        send_back(s, "own")
+        if s == 0:
             spread_total()
     wait_back_take(slots - 1)
     send_back(slots - 1, "mate")

time: 59.3 us -> 59.3 us (level)
  no operation moved by 1% of the time
where the time goes in v1:
time: 59.3 us; the launch traced here: 59.1 us
  Pallas kernels  58.4 us (98%)
  between operations  0.64 us (1%)
    pallas_call x1, Pallas kernels, per_device(): pl.pallas_call(functools.partial(exchange_kernel, entry_count, owners, te...  54.7 us
    pallas_call x1, Pallas kernels, per_device(): pl.pallas_call(functools.partial(finish_kernel, slots), out_shape=(jax.Sh...  3.71 us

profile of v1, /device:TPU:0, one launch (start us, length us, event | category | flops | bytes accessed | tf_op | source)
XLA Modules:
  0.0 59.1 jit_solution(4973094480840689525)
XLA Ops:
  0.6 54.7 %exchange.1 = (f32[4,512,512]{2,1,0:T(8,128)S(1)}, f32[4,512,512]{2,1,0:T(8,128)S(1)}, bf16[128,16,512]{2,1,0:T(8,128)(2,1)S(1)}, f32[1,128]{1,0:T(1,128)S(1)}) custom-call(s32[4,16]{1,0:T(4,128)} %bitcast.2, s32[4,16]{1,0:T(4,128)} %bitcast.4, f32[16,16,2048]{2,1,0:T(8,128)} %grad_hbm.1, bf16[4,512,512]{2,1,0:T(8,128)(2,1)} %lroot_hbm.1, ...), custom_call_target="tpu_custom_call" | custom-call | flops 4294967296 | bytes 25165824 | tf_op jit(solution)/shard_map/exchange/pallas_call | solution.py:342
  55.4 3.7 %finish.1 = (f32[4,512,512]{2,1,0:T(8,128)}, f32[4,512,512]{2,1,0:T(8,128)}, bf16[16,16,2048]{2,1,0:T(8,128)(2,1)}) custom-call(s32[4,16]{1,0:T(4,128)} %bitcast.3, s32[4,16]{1,0:T(4,128)} %bitcast.5, f32[4,512,512]{2,1,0:T(8,128)S(1)} %get-tuple-element.7.left, f32[4,512,512]{2,1,0:T(8,128)S(1)} %get-tuple-element.8.right, ...), custom_call_target="tpu_custom_call" | custom-call | bytes 9437184 | tf_op jit(solution)/shard_map/finish/pallas_call | solution.py:380
